TPU v7x, 128 devices: a whole 4x4x4 slice. The times are simulated.
128 devices in a mesh: scen: 4 (over x), arc: 32 (over z, y, core).
Axes of the slice: x: 4, y: 4, z: 4, core: 2. Of those that a mesh axis runs over, the one named last changes fastest.
Arguments:
- tiles: bfloat16 [65536, 128, 128], P(('scen', 'arc'))
- tile_rows: int32 [65536], P(('scen', 'arc')), may hold values from 0 to 511, as said below
- tile_cols: int32 [65536], P(('scen', 'arc')), may hold values from 0 to 31, as said below
- design: int32 [131072], P('arc'), may hold values 0 or 1
- cost: float32 [16, 131072], P('scen', 'arc')
- rhs: float32 [262144], P('scen'), may hold values from -6 to 6
- primal: float32 [16, 131072], P('scen', 'arc'), may hold values from 0 to 2
- dual: float32 [262144], P('scen'), may hold values from 0 to 1
- step_size: float32 [], replicated, may hold values from 0.3 to 0.9
Outputs:
- new_primal: float32 [16, 131072], P('scen', 'arc')
- new_dual: float32 [262144], P(('scen', 'arc'))
- movement: float32 [], replicated
- interaction: float32 [], replicated
Inputs may be any that keep to these rules, and one draw needn't show every extreme that they name: `tile_rows`: on each device the 512 blocks lie in distinct block rows, one in every block row of the device; block rows k * 128 to (k + 1) * 128 - 1 hold the device's k-th scenario. `tile_cols`: within each scenario of a device, every one of the 32 block columns holds the same number of blocks.
All inputs are finite; a program needn't handle non-finite values. No bound on the sum of `design` on one device may be relied on, other than what follows from the above.
Results may differ from a plain program's by a relative error of at most 0.0034.
Values sent between devices are 32-bit elements; how exact they have to be, the bound alone decides.
No kernel may reach another device: no remote copies, remote signals or barrier semaphores. Data moves between devices by JAX's collectives and lax.ppermute only.
A program may use at most 128 MiB of HBM per device.

v0:
```python
import functools

import jax
import jax.numpy as jnp
from jax import lax
from jax.experimental import pallas as pl
from jax.experimental.pallas import tpu as pltpu
from jax.sharding import PartitionSpec as P

TILE = 128
PER_COPY = 4
CHUNK = 64
RING = 3
STEP = 32
CORE = 2
F32 = jnp.float32
BF16 = jnp.bfloat16


def peak(block):
    parts = [jnp.abs(block[k : k + 16]) for k in range(0, block.shape[0], 16)]
    while len(parts) > 1:
        parts = [jnp.maximum(a, b) for a, b in zip(parts[::2], parts[1::2])]
    return jnp.max(parts[0].astype(F32), axis=0, keepdims=True)


def bits(size):
    assert size & (size - 1) == 0
    return size.bit_length() - 1


def pieces_of(ref, share):
    return [ref[k : k + share, :] for k in range(0, ref.shape[0], share)]


def by_scen(ref, scen_dev):
    size = ref.shape[0] // scen_dev
    return [ref[k * size : (k + 1) * size, :] for k in range(scen_dev)]


def add(parts):
    return functools.reduce(jnp.add, parts)


def high(parts):
    return functools.reduce(jnp.maximum, parts)


def split_cores(rows, keep, give, share, me, part=0, parts=1):
    for chip in range(rows.shape[0] // (CORE * share)):
        to = (chip * parts + part) * share
        for ref, core in ((keep, me & 1), (give, 1 - (me & 1))):
            start = pl.multiple_of((chip * CORE + core) * share, share)
            ref[to : to + share, :] = rows[pl.ds(start, share), :]


def first_kernel(
    n_scen, n_arc, rows_hbm, cols_hbm, tiles, dual_hbm, rhs_hbm, cost_hbm, primal_hbm,
    turned, slot_rows, keep, give, col_peak, gap, cost, primal, send, own_dual, own_rhs,
    ring, sems, seen, row_peak, dual, rows, cols, cost_flat, primal_flat, more,
):
    count = tiles.shape[0]
    copies = col_peak.shape[0]
    scen_dev = cost_flat.shape[0]
    col_tiles = copies // scen_dev
    row_tiles = dual.shape[0]
    per_scen = row_tiles // scen_dev
    share = row_tiles // n_arc
    chunks = count // CHUNK
    me = lax.axis_index("arc")

    def fetch(chunk):
        slot = lax.rem(chunk, RING)
        return pltpu.make_async_copy(
            tiles.at[pl.ds(chunk * CHUNK, CHUNK)], ring.at[slot], sems.at[slot]
        )

    mine = pl.ds(me * share, share)
    others = [
        pltpu.make_async_copy(dual_hbm, dual, more.at[0]),
        pltpu.make_async_copy(dual_hbm.at[mine], own_dual, more.at[1]),
        pltpu.make_async_copy(rhs_hbm.at[mine], own_rhs, more.at[2]),
        pltpu.make_async_copy(rows_hbm, rows, more.at[3]),
        pltpu.make_async_copy(cols_hbm, cols, more.at[4]),
        pltpu.make_async_copy(cost_hbm, cost_flat, more.at[5]),
        pltpu.make_async_copy(primal_hbm, primal_flat, more.at[6]),
    ]
    for copy in others:
        copy.start()
    for chunk in range(RING - 1):
        fetch(chunk).start()

    col_peak[...] = jnp.zeros_like(col_peak)
    gap[...] = jnp.zeros_like(gap)
    @pl.loop(0, copies)
    def _(copy):
        seen[copy] = 0

    for copy in others:
        copy.wait()
    for s in range(scen_dev):
        for c in range(col_tiles):
            at, to = slice(c * TILE, (c + 1) * TILE), s * col_tiles + c
            cost[to : to + 1, :] = cost_flat[s : s + 1, at]
            primal[to : to + 1, :] = primal_flat[s : s + 1, at]

    def one(k, block):
        r = rows[k]
        copy = ((r >> bits(per_scen)) << bits(col_tiles)) + cols[k]
        nth = seen[copy]
        seen[copy] = nth + 1
        slot_rows[copy * PER_COPY + nth] = r
        here = pl.ds(copy, 1)
        col_peak[here, :] = jnp.maximum(col_peak[here, :], peak(block))
        picked = jnp.broadcast_to(dual[pl.ds(r, 1), :], (16, TILE)).astype(BF16)
        gap[here, :] += jnp.dot(picked, block, preferred_element_type=F32)[:1]
        block = jnp.transpose(block)
        turned[copy, :, pl.ds(pl.multiple_of(nth * TILE, TILE), TILE)] = block
        row_peak[pl.ds(r, 1), :] = peak(block)

    @pl.loop(0, chunks)
    def _(chunk):
        fetch(chunk).wait()

        @pl.when(chunk + RING - 1 < chunks)
        def _():
            fetch(chunk + RING - 1).start()

        slot = lax.rem(chunk, RING)
        for at in range(CHUNK):
            one(chunk * CHUNK + at, ring[slot, at])

    split_cores(row_peak, keep, give, share, me)
    gap[...] = cost[...] - gap[...]
    scenarios = scen_dev * n_scen
    send[:col_tiles, :] = high(by_scen(col_peak, scen_dev))
    send[col_tiles : 2 * col_tiles, :] = add([g / scenarios for g in by_scen(gap, scen_dev)])
    send[2 * col_tiles :, :] = add([p / scenarios for p in by_scen(primal, scen_dev)])


def each_copy(copies, one):
    @pl.loop(0, copies // STEP)
    def _(step):
        for u in range(STEP):
            one(step * STEP + u)


def joined(parts, rows, tops):
    join = lambda f: f(f(parts[0][rows, :], parts[2][rows, :]), f(parts[1][rows, :], parts[3][rows, :]))
    return join(jnp.maximum if rows.stop <= tops else jnp.add)


def row_kernel(
    rows, turned, own_scale, col_peak, design, own, first, third, second,
    keep, give, col_scale, means, row_high,
):
    copies = col_peak.shape[0]
    col_tiles = design.shape[0]
    parts = (own, first, second, third)
    shared = joined(parts, slice(0, col_tiles), col_tiles)
    for k in range(2):
        at = slice((k + 1) * col_tiles, (k + 2) * col_tiles)
        means[k * col_tiles : (k + 1) * col_tiles, :] = joined(parts, at, col_tiles)
    is_design = design[...] == 1
    for s in range(copies // col_tiles):
        at = slice(s * col_tiles, (s + 1) * col_tiles)
        col_scale[at, :] = 1.0 / jnp.sqrt(jnp.where(is_design, shared, col_peak[at, :]))

    def one(copy):
        spread = jnp.transpose(jnp.broadcast_to(col_scale[pl.ds(copy, 1), :], (TILE, TILE)))
        for b in range(PER_COPY):
            block = jnp.abs(turned[copy, :, b * TILE : (b + 1) * TILE].astype(F32))
            here = pl.ds(rows[copy * PER_COPY + b], 1)
            row_high[here, :] = jnp.max(block * spread, axis=0, keepdims=True)

    each_copy(copies, one)
    share = own_scale.shape[0]
    split_cores(row_high, keep, give, share, lax.axis_index("arc"))
    give[keep.shape[0] :, :] = own_scale[...]


def col_kernel(
    rows, turned, gathered, own_scale, own_rhs, col_scale, cost, design,
    col_peak, send, own_row, row_scale,
):
    share = own_scale.shape[0]
    me = lax.axis_index("arc")
    pieces = pieces_of(gathered, share)
    for chip in range(len(pieces) // (CORE + 1)):
        for piece, core in zip(pieces[chip * (CORE + 1) :], (me & 1, 1 - (me & 1))):
            first = pl.multiple_of((chip * CORE + core) * share, share)
            row_scale[pl.ds(first, share), :] = piece
    own = own_scale[...]
    own = own / jnp.sqrt(own * high(pieces[CORE :: CORE + 1]))
    own_row[...] = own

    def one(copy):
        best = None
        for b in range(PER_COPY):
            scale = row_scale[pl.ds(rows[copy * PER_COPY + b], 1), :]
            part = jnp.abs(turned[copy, :, b * TILE : (b + 1) * TILE].astype(F32)) * scale
            best = part if best is None else jnp.maximum(best, part)
        here = pl.ds(copy, 1)
        top = jnp.max(jnp.transpose(best), axis=0, keepdims=True)
        col_peak[here, :] = col_scale[here, :] * top

    each_copy(turned.shape[0], one)
    col_tiles = design.shape[0]
    is_design = design[...] == 1
    scen_dev = col_peak.shape[0] // col_tiles
    peaks = by_scen(col_peak, scen_dev)
    send[:col_tiles, :] = high(peaks)
    scaled = [
        (jnp.where(is_design, scale, scale / jnp.sqrt(p)) * c) ** 2
        for scale, p, c in zip(by_scen(col_scale, scen_dev), peaks, by_scen(cost, scen_dev))
    ]
    send[col_tiles : 2 * col_tiles, :] = add(scaled)
    right = (own * own_rhs[...]) ** 2
    send[2 * col_tiles :, :] = add([right[k : k + 8] for k in range(0, share, 8)])


def lanes(terms):
    lane = lax.broadcasted_iota(jnp.int32, (1, TILE), 1)
    row = jnp.zeros((1, TILE), F32)
    for k, term in enumerate(terms):
        row = jnp.where(lane == k, jnp.sum(term, axis=1, keepdims=True), row)
    return row


def norm_kernel(design, own, first, third, second, shared, send):
    col_tiles = design.shape[0]
    parts = (own, first, second, third)
    tops = joined(parts, slice(0, col_tiles), col_tiles)
    shared[...] = tops
    squares = joined(parts, slice(col_tiles, 2 * col_tiles), col_tiles)
    squares = jnp.where(design[...] == 1, squares / tops, squares)
    right = joined(parts, slice(2 * col_tiles, 2 * col_tiles + 8), col_tiles)
    rows = [jnp.sum(t, axis=0, keepdims=True) for t in (squares, right)]
    send[...] = jnp.broadcast_to(lanes(rows), send.shape)


def image_kernel(
    share, rows, turned, step_size, totals, col_peak, shared, col_scale, gap, means, primal, design,
    keep, give, new_primal, scalars, step, image, old,
):
    col_tiles = design.shape[0]
    copies = gap.shape[0]
    is_design = design[...] == 1
    total = jnp.sum(totals[...], axis=0, keepdims=True)
    cost_total, rhs_total = total[:, :1], total[:, 1:2]
    omega = jnp.sqrt(cost_total + 1e-06) / jnp.sqrt(rhs_total + 1e-06)
    tau = step_size[:, :1] / omega
    mean_gap = means[:col_tiles, :]
    mean_primal = means[col_tiles:, :]
    moved = None
    for s in range(copies // col_tiles):
        at = slice(s * col_tiles, (s + 1) * col_tiles)
        top = jnp.where(is_design, shared[...], col_peak[at, :])
        scale = col_scale[at, :] / jnp.sqrt(top)
        weight = tau * scale * scale
        here = primal[at, :]
        half = jnp.where(is_design, mean_primal, here) - weight * jnp.where(
            is_design, mean_gap, gap[at, :]
        )
        new = jnp.maximum(half, 0.0)
        step[at, :] = new - here
        square = ((new - here) / scale) ** 2
        moved = square if moved is None else moved + square
        for c in range(col_tiles):
            new_primal[s : s + 1, c * TILE : (c + 1) * TILE] = new[c : c + 1, :]
    scalars[:1, :] = jnp.broadcast_to(omega, (1, TILE))
    scalars[1:2, :] = jnp.sum(moved, axis=0, keepdims=True)

    def one(copy):
        here = pl.ds(copy, 1)
        values = [jnp.broadcast_to(v[here, :], (8, TILE)) for v in (step, primal)]
        values = jnp.concatenate(values, axis=0).astype(BF16)
        out = jnp.dot(values, turned[copy], preferred_element_type=F32)
        for b in range(PER_COPY):
            here, at = pl.ds(rows[copy * PER_COPY + b], 1), slice(b * TILE, (b + 1) * TILE)
            image[here, :] = out[:1, at]
            old[here, :] = out[8:9, at]

    each_copy(copies, one)
    me = lax.axis_index("arc")
    split_cores(image, keep, give, share, me, 0, 2)
    split_cores(old, keep, give, share, me, 1, 2)


def dual_kernel(step_size, scalars, images, own_row, own_rhs, dual, new_dual, send):
    omega = scalars[:1, :]
    sigma = step_size[...] * omega
    scale = own_row[...]
    pieces = pieces_of(images, scale.shape[0])
    step_image, old = add(pieces[::2]), add(pieces[1::2])
    new = jnp.maximum(
        dual[...] + sigma * scale * scale * (own_rhs[...] - old - 2.0 * step_image), 0.0
    )
    step = new - dual[...]
    new_dual[...] = new
    moved = jnp.sum((step / scale) ** 2, axis=0, keepdims=True)
    terms = (
        omega * scalars[1:2, :] + moved / omega,
        jnp.sum(step * step_image, axis=0, keepdims=True),
    )
    send[...] = jnp.broadcast_to(lanes(terms), send.shape)


VMEM = pl.BlockSpec(memory_space=pltpu.VMEM)
SMEM = pl.BlockSpec(memory_space=pltpu.SMEM)
HBM = pl.BlockSpec(memory_space=pltpu.HBM)
LIMIT = 20 * 1024 * 1024


def f32(*shape):
    return jax.ShapeDtypeStruct(shape, F32)


def start(n_scen, n_arc, rows, cols, tiles, dual, rhs, cost, primal):
    copies = cost.size // TILE
    col_tiles = copies // cost.shape[0]
    share = dual.shape[0] // n_arc
    slots = jax.ShapeDtypeStruct(rows.shape, jnp.int32)
    wide = f32(copies, TILE)
    own = f32(share, TILE)
    half = f32(dual.shape[0] // CORE, TILE)
    return pl.pallas_call(
        functools.partial(first_kernel, n_scen, n_arc),
        out_shape=[
            pltpu.VMEM((copies, TILE, PER_COPY * TILE), BF16),
            slots,
            half,
            half,
            wide,
            wide,
            wide,
            wide,
            f32(3 * col_tiles, TILE),
            own,
            own,
        ],
        in_specs=[HBM] * 7,
        out_specs=[VMEM, SMEM] + [VMEM] * 9,
        scratch_shapes=[
            pltpu.VMEM((RING, CHUNK, TILE, TILE), BF16),
            pltpu.SemaphoreType.DMA((RING,)),
            pltpu.SMEM((copies,), jnp.int32),
            pltpu.VMEM(dual.shape, F32),
            pltpu.VMEM(dual.shape, F32),
            pltpu.SMEM(rows.shape, jnp.int32),
            pltpu.SMEM(cols.shape, jnp.int32),
            pltpu.VMEM(cost.shape, F32),
            pltpu.VMEM(primal.shape, F32),
            pltpu.SemaphoreType.DMA((7,)),
        ],
        compiler_params=pltpu.CompilerParams(vmem_limit_bytes=LIMIT),
    )(
        *[
            pltpu.with_memory_space_constraint(a, pltpu.HBM)
            for a in (rows, cols, tiles, dual, rhs, cost, primal)
        ]
    )


def again(kernel, outs, scalars, turned, *vectors, scratch=()):
    specs = [SMEM] * len(scalars)
    if turned is not None:
        vectors = (pltpu.with_memory_space_constraint(turned, pltpu.VMEM), *vectors)
    return pl.pallas_call(
        kernel,
        out_shape=outs,
        in_specs=specs + [VMEM] * len(vectors),
        out_specs=[VMEM] * len(outs),
        scratch_shapes=scratch,
        compiler_params=pltpu.CompilerParams(vmem_limit_bytes=LIMIT),
        cost_estimate=pl.CostEstimate(
            flops=7 * 10**9 if turned is not None else 10**6, bytes_accessed=2**20, transcendentals=0
        ),
    )(*scalars, *vectors)


def swap_core(values):
    n = lax.axis_size("arc")
    return lax.ppermute(values, "arc", [(i, i ^ 1) for i in range(n)])


def exchange(values):
    n = lax.axis_size("arc")
    groups = [[*range(c, n, CORE)] for c in range(CORE)]
    return lax.all_to_all(values, "arc", 0, 0, axis_index_groups=groups, tiled=True)


def with_scen(values):
    n = lax.axis_size("scen")
    shifts = [[(i, (i - k) % n) for i in range(n)] for k in (1, 3, 2)]
    return [values] + [lax.ppermute(values, "scen", pairs) for pairs in shifts]


def per_device(tiles, tile_rows, tile_cols, design, cost, rhs, primal, dual, step_size):
    tile = tiles.shape[1]
    scen_dev, cols_dev = primal.shape
    col_tiles = cols_dev // tile
    row_tiles = dual.shape[0] // tile
    copies = scen_dev * col_tiles
    n_scen, n_arc = lax.axis_size("scen"), lax.axis_size("arc")
    share = row_tiles // n_arc
    chips = n_arc // CORE
    wide = f32(copies, tile)
    tall = f32(row_tiles, tile)
    own = f32(share, tile)
    design = design.reshape(col_tiles, tile)
    step_size, cost = lax.optimization_barrier((jnp.full((1, tile), step_size), cost))

    (
        turned, slot_rows, keep, give, col_peak, gap, cost, primal, send, own_dual, own_rhs
    ) = start(
        n_scen, n_arc, tile_rows, tile_cols, tiles,
        dual.reshape(row_tiles, tile), rhs.reshape(row_tiles, tile), cost, primal,
    )
    sends = with_scen(send)
    near, sends = lax.optimization_barrier((swap_core(give), sends))
    reduced = exchange(jnp.maximum(keep, near).reshape(chips, share, tile))
    own_scale = 1.0 / jnp.sqrt(high([*reduced]))
    own_scale, col_peak = lax.optimization_barrier((own_scale, col_peak))
    half = f32(row_tiles // CORE, tile)
    keep, give, col_scale, means = again(
        row_kernel, [half, f32(half.shape[0] + share, tile), wide, f32(2 * col_tiles, tile)],
        [slot_rows], turned, own_scale, col_peak, design, *sends,
        scratch=[pltpu.VMEM(tall.shape, F32)],
    )
    near = swap_core(give)
    row_high = jnp.maximum(keep, near[: half.shape[0]]).reshape(chips, share, tile)
    scales = [
        jnp.broadcast_to(v[None], row_high.shape) for v in (own_scale, near[half.shape[0] :])
    ]
    gathered = exchange(jnp.stack((*scales, row_high), axis=1))
    col_peak, send, own_row = again(
        col_kernel, [wide, f32(2 * col_tiles + 8, tile), own], [slot_rows],
        turned, gathered.reshape(-1, tile), own_scale, own_rhs, col_scale, cost, design,
        scratch=[pltpu.VMEM(tall.shape, F32)],
    )
    shared, send = again(
        norm_kernel, [f32(col_tiles, tile), f32(n_arc, tile)], [], None, design, *with_scen(send)
    )
    totals = lax.all_to_all(send, "arc", 0, 0, tiled=True)

    keep, give, new_primal, scalars = again(
        functools.partial(image_kernel, share),
        [tall, tall, f32(scen_dev, cols_dev), f32(8, tile)], [slot_rows],
        turned, step_size, totals, col_peak, shared, col_scale, gap, means, primal, design,
        scratch=[pltpu.VMEM(a.shape, F32) for a in (wide, tall, tall)],
    )
    images = exchange((keep + swap_core(give)).reshape(chips, 2 * share, tile))
    new_dual, send = again(
        dual_kernel, [own, f32(n_scen * n_arc, tile)], [], None,
        step_size, scalars, images.reshape(row_tiles, tile), own_row, own_rhs, own_dual,
    )
    sums = jnp.sum(lax.all_to_all(send, ("scen", "arc"), 0, 0, tiled=True), axis=0)
    return (new_primal, new_dual.reshape(share * tile), sums[0], sums[1])


def solution(mesh):
    placed = (
        P(("scen", "arc"), None, None),
        P(("scen", "arc")),
        P(("scen", "arc")),
        P("arc"),
        P("scen", "arc"),
        P("scen"),
        P("scen", "arc"),
        P("scen"),
        P(),
    )
    return jax.shard_map(
        per_device,
        mesh=mesh,
        in_specs=placed,
        out_specs=(P("scen", "arc"), P(("scen", "arc")), P(), P()),
        check_vma=False,
    )
```

profile of v0, /device:TPU:1, one launch (start us, length us, event | category | flops | bytes accessed | tf_op | source)
XLA Modules:
  0.0 113.9 jit_solution(2790899328514923084)
XLA Ops:
  0.6 0.0 copy-start
  1.3 10.1 %shard_map.120 = (bf16[128,128,512]{2,1,0:T(8,128)(2,1)S(1)}, s32[512]{0:T(512)S(1)}, f32[256,128]{1,0:T(8,128)S(1)}, f32[256,128]{1,0:T(8,128)S(1)}, f32[128,12...) custom-call(s32[512]{0:T(512)} %rows_hbm.1, ...), custom_call_target="tpu_custom_call" | custom-call | tf_op jit(solution)/shard_map/pallas_call | solution.py:327
  11.4 1.8 %collective-permute-start = (f32[256,128]{1,0:T(8,128)S(1)}, f32[256,128]{1,0:T(8,128)S(1)}, u32[]{:S(2)}, u32[]{:S(2)}) collective-permute-start(f32[256,128]{1,0:T(8,128)S(1)} %get-tuple-element.44), channel_id=1, source_target_pairs={{0,1},{1,0},{2,3},{3,2},{4,5},{5,4},{6,7},{7,6},{8,9},{9,8},{10,11... | collective-permute-start | bytes 393224 | tf_op jit(solution)/shard_map/ppermute | solution.py:384
  13.2 2.8 %collective-permute-start.3 = (f32[96,128]{1,0:T(8,128)S(1)}, f32[96,128]{1,0:T(8,128)S(1)}, u32[]{:S(2)}, u32[]{:S(2)}) collective-permute-start(f32[96,128]{1,0:T(8,128)S(1)} %get-tuple-element.50.own), channel_id=1, source_target_pairs={{0,64},{32,96},{64,0},{96,32},{1,65},{33,97},{65,1},{97,33},{2,66}... | collective-permute-start | bytes 147464 | tf_op jit(solution)/shard_map/ppermute | solution.py:396
  16.1 0.3 collective-permute-start.2
  16.4 2.4 %collective-permute-start.1 = (f32[96,128]{1,0:T(8,128)S(1)}, f32[96,128]{1,0:T(8,128)S(1)}, u32[]{:S(2)}, u32[]{:S(2)}) collective-permute-start(f32[96,128]{1,0:T(8,128)S(1)} %get-tuple-element.50.own), channel_id=1, source_target_pairs={{0,96},{32,0},{64,32},{96,64},{1,97},{33,1},{65,33},{97,65},{2,98}... | collective-permute-start | bytes 147464 | tf_op jit(solution)/shard_map/ppermute | solution.py:396
  18.8 0.0 collective-permute-done.3.second
  18.8 1.5 %collective-permute-done.2.third = f32[96,128]{1,0:T(8,128)S(1)} collective-permute-done((f32[96,128]{1,0:T(8,128)S(1)}, f32[96,128]{1,0:T(8,128)S(1)}, u32[]{:S(2)}, u32[]{:S(2)}) %collective-permute-start.2) | collective-permute-done | bytes 49184 | tf_op jit(solution)/shard_map/ppermute | solution.py:396
  20.2 0.0 collective-permute-done.1.first
  20.2 0.0 collective-permute-done
  20.3 14.1 %all_to_all.35 = f32[16,16,128]{2,1,0:T(8,128)S(1)} all-to-all(f32[16,16,128]{2,1,0:T(8,128)S(1)} %bitcast.32), channel_id=1, replica_groups={{0,2,4,6,8,10,12,14,16,18,20,22,24,26,28,30},{1,3,5,7,9,11,13,15,17,19,..., dimensions={0} | all-to-all | bytes 262144 | tf_op jit(solution)/shard_map/all_to_all | solution.py:390
  34.4 0.0 copy-done
  34.4 5.4 %shard_map.121 = (f32[256,128]{1,0:T(8,128)S(1)}, f32[272,128]{1,0:T(8,128)S(1)}, f32[128,128]{1,0:T(8,128)S(1)}, f32[64,128]{1,0:T(8,128)S(1)}) custom-call(s32[512]{0:T(512)S(1)} %get-tuple-element.40.rows, bf16[128,128,512]{2,1,0:T(8,128)(2,1)S(1)} %get-tuple-element.41.turned, f32[16,128]{1,0:T(8,128)S(1)} %fusion.1.own_scale, ...), custom_call_target="tpu_custom_call" | custom-call | flops 7000000000 | bytes 1048576 | tf_op jit(solution)/shard_map/pallas_call | solution.py:369
  39.7 3.0 %collective-permute-start.4 = (f32[272,128]{1,0:T(8,128)S(1)}, f32[272,128]{1,0:T(8,128)S(1)}, u32[]{:S(2)}, u32[]{:S(2)}) collective-permute-start(f32[272,128]{1,0:T(8,128)S(1)} %get-tuple-element.54), channel_id=1, source_target_pairs={{0,1},{1,0},{2,3},{3,2},{4,5},{5,4},{6,7},{7,6},{8,9},{9,8},{10,11... | collective-permute-start | bytes 417800 | tf_op jit(solution)/shard_map/ppermute | solution.py:384
  42.8 1.0 collective-permute-done.4
  43.9 12.3 %all_to_all.36 = f32[16,3,16,128]{3,2,1,0:T(8,128)S(1)} all-to-all(f32[16,3,16,128]{3,2,1,0:T(8,128)S(1)} %pad_maximum_fusion), channel_id=1, replica_groups={{0,2,4,6,8,10,12,14,16,18,20,22,24,26,28,30},{1,3,5,7,9,11,13,15,17,19,..., dimensions={0} | all-to-all | bytes 786432 | tf_op jit(solution)/shard_map/all_to_all | solution.py:390
  56.2 5.4 %shard_map.122 = (f32[128,128]{1,0:T(8,128)S(1)}, f32[72,128]{1,0:T(8,128)S(1)}, f32[16,128]{1,0:T(8,128)S(1)}) custom-call(s32[512]{0:T(512)S(1)} %get-tuple-element.40.rows, bf16[128,128,512]{2,1,0:T(8,128)(2,1)S(1)} %get-tuple-element.41.turned, f32[768,128]{1,0:T(8,128)S(1)} %bitcast.23, f32[16,128]{1,0:T(8,128)S(1)} %fusion.1.own_scale, ...), custom_call_target="tpu_custom_call" | custom-call | flops 7000000000 | bytes 1048576 | tf_op jit(solution)/shard_map/pallas_call | solution.py:369
  61.6 1.3 %collective-permute-start.7 = (f32[72,128]{1,0:T(8,128)S(1)}, f32[72,128]{1,0:T(8,128)S(1)}, u32[]{:S(2)}, u32[]{:S(2)}) collective-permute-start(f32[72,128]{1,0:T(8,128)S(1)} %get-tuple-element.59.own), channel_id=1, source_target_pairs={{0,64},{32,96},{64,0},{96,32},{1,65},{33,97},{65,1},{97,33},{2,66}... | collective-permute-start | bytes 110600 | tf_op jit(solution)/shard_map/ppermute | solution.py:396
  62.8 2.4 %collective-permute-start.6 = (f32[72,128]{1,0:T(8,128)S(1)}, f32[72,128]{1,0:T(8,128)S(1)}, u32[]{:S(2)}, u32[]{:S(2)}) collective-permute-start(f32[72,128]{1,0:T(8,128)S(1)} %get-tuple-element.59.own), channel_id=1, source_target_pairs={{0,32},{32,64},{64,96},{96,0},{1,33},{33,65},{65,97},{97,1},{2,34}... | collective-permute-start | bytes 110600 | tf_op jit(solution)/shard_map/ppermute | solution.py:396
  65.2 0.3 collective-permute-start.5
  65.5 0.5 collective-permute-done.7.second
  65.9 0.9 collective-permute-done.6.third
  66.8 1.4 %collective-permute-done.5.first = f32[72,128]{1,0:T(8,128)S(1)} collective-permute-done((f32[72,128]{1,0:T(8,128)S(1)}, f32[72,128]{1,0:T(8,128)S(1)}, u32[]{:S(2)}, u32[]{:S(2)}) %collective-permute-start.5) | collective-permute-done | bytes 36896 | tf_op jit(solution)/shard_map/ppermute | solution.py:396
  68.2 0.1 shard_map.123
  68.3 12.9 %all_to_all.37 = f32[32,1,128]{2,1,0:T(1,128)S(1)} all-to-all(f32[32,1,128]{2,1,0:T(1,128)S(1)} %bitcast.30), channel_id=1, replica_groups=mesh['scen'=4,'arc'=32] {'arc'}, dimensions={0} | all-to-all | bytes 32768 | tf_op jit(solution)/shard_map/all_to_all | solution.py:445
  81.2 4.0 %shard_map.124 = (f32[512,128]{1,0:T(8,128)S(1)}, f32[512,128]{1,0:T(8,128)S(1)}, f32[4,4096]{1,0:T(4,128)}, f32[8,128]{1,0:T(8,128)S(1)}) custom-call(s32[512]{0:T(512)S(1)} %get-tuple-element.40.rows, bf16[128,128,512]{2,1,0:T(8,128)(2,1)S(1)} %get-tuple-element.41.turned, f32[1,128]{1,0:T(1,128)S(1)} %broadcast_in_dim.2.step_size, ...), custom_call_target="tpu_custom_call" | custom-call | flops 7000000000 | bytes 1048576 | tf_op jit(solution)/shard_map/pallas_call | solution.py:369
  85.2 0.6 collective-permute-start.8
  85.9 1.2 %collective-permute-done.8 = f32[512,128]{1,0:T(8,128)S(1)} collective-permute-done((f32[512,128]{1,0:T(8,128)S(1)}, f32[512,128]{1,0:T(8,128)S(1)}, u32[]{:S(2)}, u32[]{:S(2)}) %collective-permute-start.8) | collective-permute-done | bytes 262176 | tf_op jit(solution)/shard_map/ppermute | solution.py:384
  87.1 10.9 %all_to_all.38 = f32[16,32,128]{2,1,0:T(8,128)S(1)} all-to-all(f32[16,32,128]{2,1,0:T(8,128)S(1)} %bitcast.31), channel_id=1, replica_groups={{0,2,4,6,8,10,12,14,16,18,20,22,24,26,28,30},{1,3,5,7,9,11,13,15,17,19,..., dimensions={0} | all-to-all | bytes 524288 | tf_op jit(solution)/shard_map/all_to_all | solution.py:390
  97.9 0.6 shard_map.125
  98.6 14.7 %all_to_all.39 = f32[128,1,128]{2,1,0:T(1,128)S(1)} all-to-all(f32[128,1,128]{2,1,0:T(1,128)S(1)} %bitcast.24), channel_id=1, replica_groups=mesh['scen'=4,'arc'=32] {'scen','arc'}, dimensions={0} | all-to-all | bytes 131072 | tf_op jit(solution)/shard_map/all_to_all | solution.py:458
  113.2 0.2 reduce_sum.9
  113.4 0.6 fusion.2
  (9 shorter events, 0.1 us)
Async XLA Ops:
  0.6 33.7 %copy-start = (s32[4096]{0:T(1024)S(1)}, s32[4096]{0:T(1024)}, u32[]{:S(2)}) copy-start(s32[4096]{0:T(1024)} %param.12) | copy-start | bytes 49156
  11.4 8.8 %collective-permute-start = (f32[256,128]{1,0:T(8,128)S(1)}, f32[256,128]{1,0:T(8,128)S(1)}, u32[]{:S(2)}, u32[]{:S(2)}) collective-permute-start(f32[256,128]{1,0:T(8,128)S(1)} %get-tuple-element.44), channel_id=1, source_target_pairs={{0,1},{1,0},{2,3},{3,2},{4,5},{5,4},{6,7},{7,6},{8,9},{9,8},{10,11... | collective-permute-start | bytes 393224 | tf_op jit(solution)/shard_map/ppermute | solution.py:384
  13.2 5.5 %collective-permute-start.3 = (f32[96,128]{1,0:T(8,128)S(1)}, f32[96,128]{1,0:T(8,128)S(1)}, u32[]{:S(2)}, u32[]{:S(2)}) collective-permute-start(f32[96,128]{1,0:T(8,128)S(1)} %get-tuple-element.50.own), channel_id=1, source_target_pairs={{0,64},{32,96},{64,0},{96,32},{1,65},{33,97},{65,1},{97,33},{2,66}... | collective-permute-start | bytes 147464 | tf_op jit(solution)/shard_map/ppermute | solution.py:396
  16.1 4.2 %collective-permute-start.2 = (f32[96,128]{1,0:T(8,128)S(1)}, f32[96,128]{1,0:T(8,128)S(1)}, u32[]{:S(2)}, u32[]{:S(2)}) collective-permute-start(f32[96,128]{1,0:T(8,128)S(1)} %get-tuple-element.50.own), channel_id=1, source_target_pairs={{0,32},{32,64},{64,96},{96,0},{1,33},{33,65},{65,97},{97,1},{2,34}... | collective-permute-start | bytes 147464 | tf_op jit(solution)/shard_map/ppermute | solution.py:396
  16.4 3.9 %collective-permute-start.1 = (f32[96,128]{1,0:T(8,128)S(1)}, f32[96,128]{1,0:T(8,128)S(1)}, u32[]{:S(2)}, u32[]{:S(2)}) collective-permute-start(f32[96,128]{1,0:T(8,128)S(1)} %get-tuple-element.50.own), channel_id=1, source_target_pairs={{0,96},{32,0},{64,32},{96,64},{1,97},{33,1},{65,33},{97,65},{2,98}... | collective-permute-start | bytes 147464 | tf_op jit(solution)/shard_map/ppermute | solution.py:396
  39.7 4.0 %collective-permute-start.4 = (f32[272,128]{1,0:T(8,128)S(1)}, f32[272,128]{1,0:T(8,128)S(1)}, u32[]{:S(2)}, u32[]{:S(2)}) collective-permute-start(f32[272,128]{1,0:T(8,128)S(1)} %get-tuple-element.54), channel_id=1, source_target_pairs={{0,1},{1,0},{2,3},{3,2},{4,5},{5,4},{6,7},{7,6},{8,9},{9,8},{10,11... | collective-permute-start | bytes 417800 | tf_op jit(solution)/shard_map/ppermute | solution.py:384
  61.6 4.4 %collective-permute-start.7 = (f32[72,128]{1,0:T(8,128)S(1)}, f32[72,128]{1,0:T(8,128)S(1)}, u32[]{:S(2)}, u32[]{:S(2)}) collective-permute-start(f32[72,128]{1,0:T(8,128)S(1)} %get-tuple-element.59.own), channel_id=1, source_target_pairs={{0,64},{32,96},{64,0},{96,32},{1,65},{33,97},{65,1},{97,33},{2,66}... | collective-permute-start | bytes 110600 | tf_op jit(solution)/shard_map/ppermute | solution.py:396
  62.8 4.0 %collective-permute-start.6 = (f32[72,128]{1,0:T(8,128)S(1)}, f32[72,128]{1,0:T(8,128)S(1)}, u32[]{:S(2)}, u32[]{:S(2)}) collective-permute-start(f32[72,128]{1,0:T(8,128)S(1)} %get-tuple-element.59.own), channel_id=1, source_target_pairs={{0,32},{32,64},{64,96},{96,0},{1,33},{33,65},{65,97},{97,1},{2,34}... | collective-permute-start | bytes 110600 | tf_op jit(solution)/shard_map/ppermute | solution.py:396
  65.2 3.1 %collective-permute-start.5 = (f32[72,128]{1,0:T(8,128)S(1)}, f32[72,128]{1,0:T(8,128)S(1)}, u32[]{:S(2)}, u32[]{:S(2)}) collective-permute-start(f32[72,128]{1,0:T(8,128)S(1)} %get-tuple-element.59.own), channel_id=1, source_target_pairs={{0,96},{32,0},{64,32},{96,64},{1,97},{33,1},{65,33},{97,65},{2,98}... | collective-permute-start | bytes 110600 | tf_op jit(solution)/shard_map/ppermute | solution.py:396
  85.2 1.8 %collective-permute-start.8 = (f32[512,128]{1,0:T(8,128)S(1)}, f32[512,128]{1,0:T(8,128)S(1)}, u32[]{:S(2)}, u32[]{:S(2)}) collective-permute-start(f32[512,128]{1,0:T(8,128)S(1)} %get-tuple-element.69), channel_id=1, source_target_pairs={{0,1},{1,0},{2,3},{3,2},{4,5},{5,4},{6,7},{7,6},{8,9},{9,8},{10,11... | collective-permute-start | bytes 786440 | tf_op jit(solution)/shard_map/ppermute | solution.py:384
where the time goes:
time: 114 us
  blocking collectives  64.8 us (57%)
  Pallas kernels  25.6 us (22%)
  starting transfers between devices  15 us (13%)
  waiting for transfers between devices  6.37 us (6%)
  between operations  1.39 us (1%)
    all_to_all x3, blocking collectives, exchange(): lax.all_to_all(values, 'arc', 0, 0, axis_index_groups=groups, tiled=True)  37.2 us
    pallas_call x5, Pallas kernels, again(): pl.pallas_call(kernel, out_shape=outs, in_specs=specs + [VMEM] * len(vect...  15.5 us
    all_to_all x1, blocking collectives, per_device(): lax.all_to_all(send, ('scen', 'arc'), 0, 0, tiled=True)  14.7 us
    all_to_all x1, blocking collectives, per_device(): totals = lax.all_to_all(send, 'arc', 0, 0, tiled=True)  12.9 us
    pallas_call x1, Pallas kernels, start(): pl.pallas_call(functools.partial(first_kernel, n_scen, n_arc), out_shape=...  10.1 us
    ppermute x6, starting transfers between devices, with_scen(): return [values] + [lax.ppermute(values, 'scen', pairs) for pairs in shifts]  9.46 us
    ppermute x3, starting transfers between devices, swap_core(): return lax.ppermute(values, 'arc', [(i, i ^ 1) for i in range(n)])  5.51 us
    ppermute x6, waiting for transfers between devices, with_scen(): return [values] + [lax.ppermute(values, 'scen', pairs) for pairs in shifts]  4.2 us
  transfers between devices with their start and end apart: 9, of which 6 were waited for; matrix products, arithmetic and copies ran while one was open for 0% of the time, Pallas kernels for 0%

commit v1 on v0

--- a/solution.py
+++ b/solution.py
@@ -227,9 +227,9 @@
     return row
 
 
-def norm_kernel(design, own, first, third, second, shared, send):
+def norm_kernel(design, gathered, shared, send):
     col_tiles = design.shape[0]
-    parts = (own, first, second, third)
+    parts = pieces_of(gathered, 2 * col_tiles + 8)
     tops = joined(parts, slice(0, col_tiles), col_tiles)
     shared[...] = tops
     squares = joined(parts, slice(col_tiles, 2 * col_tiles), col_tiles)
@@ -396,6 +396,12 @@
     return [values] + [lax.ppermute(values, "scen", pairs) for pairs in shifts]
 
 
+def all_scen(values):
+    n = lax.axis_size("scen")
+    spread = jnp.broadcast_to(values[None], (n, *values.shape))
+    return lax.all_to_all(spread, "scen", 0, 0, tiled=True).reshape(-1, values.shape[1])
+
+
 def per_device(tiles, tile_rows, tile_cols, design, cost, rhs, primal, dual, step_size):
     tile = tiles.shape[1]
     scen_dev, cols_dev = primal.shape
@@ -440,7 +446,7 @@
         scratch=[pltpu.VMEM(tall.shape, F32)],
     )
     shared, send = again(
-        norm_kernel, [f32(col_tiles, tile), f32(n_arc, tile)], [], None, design, *with_scen(send)
+        norm_kernel, [f32(col_tiles, tile), f32(n_arc, tile)], [], None, design, all_scen(send)
     )
     totals = lax.all_to_all(send, "arc", 0, 0, tiled=True)
 

time: 114 us -> 116 us (1.018)
  blocking collectives: 64.8 us -> 73 us
  starting transfers between devices: 15 us -> 11 us
  waiting for transfers between devices: 6.37 us -> 3.64 us
    all_to_all x0 -> x1, blocking collectives: none -> 8.94 us  [all_scen(): lax.all_to_all(spread, 'scen', 0, 0, tiled=True)]
    ppermute x6 -> x3, starting transfers between devices: 9.46 us -> 5.51 us  [with_scen(): return [values] + [lax.ppermute(values, 'scen', pairs) for pairs in shifts]]
    ppermute x6 -> x3, waiting for transfers between devices: 4.2 us -> 1.48 us  [with_scen(): return [values] + [lax.ppermute(values, 'scen', pairs) for pairs in shifts]]
  transfers between devices with their start and end apart: 9 -> 6, of which waited for: 6 -> 3; matrix products, arithmetic and copies ran while one was open for 0% -> 0% of each run, Pallas kernels for 0% -> 0%
where the time goes in v1:
time: 116 us
  blocking collectives  73 us (63%)
  Pallas kernels  25.6 us (22%)
  starting transfers between devices  11 us (9%)
  waiting for transfers between devices  3.64 us (3%)
  between operations  1.39 us (1%)
    all_to_all x3, blocking collectives, exchange(): lax.all_to_all(values, 'arc', 0, 0, axis_index_groups=groups, tiled=True)  37.2 us
    pallas_call x5, Pallas kernels, again(): pl.pallas_call(kernel, out_shape=outs, in_specs=specs + [VMEM] * len(vect...  15.5 us
    all_to_all x1, blocking collectives, per_device(): lax.all_to_all(send, ('scen', 'arc'), 0, 0, tiled=True)  14 us
    all_to_all x1, blocking collectives, per_device(): totals = lax.all_to_all(send, 'arc', 0, 0, tiled=True)  12.8 us
    pallas_call x1, Pallas kernels, start(): pl.pallas_call(functools.partial(first_kernel, n_scen, n_arc), out_shape=...  10.1 us
    all_to_all x1, blocking collectives, all_scen(): lax.all_to_all(spread, 'scen', 0, 0, tiled=True)  8.94 us
    ppermute x3, starting transfers between devices, with_scen(): return [values] + [lax.ppermute(values, 'scen', pairs) for pairs in shifts]  5.51 us
    ppermute x3, starting transfers between devices, swap_core(): return lax.ppermute(values, 'arc', [(i, i ^ 1) for i in range(n)])  5.49 us
  transfers between devices with their start and end apart: 6, of which 3 were waited for; matrix products, arithmetic and copies ran while one was open for 0% of the time, Pallas kernels for 0%

profile of v1, /device:TPU:1, one launch (start us, length us, event | category | flops | bytes accessed | tf_op | source)
XLA Modules:
  0.0 115.6 jit_solution(9247525933781168145)
XLA Ops:
  0.6 0.0 copy-start
  1.3 10.1 %shard_map.120 = (bf16[128,128,512]{2,1,0:T(8,128)(2,1)S(1)}, s32[512]{0:T(512)S(1)}, f32[256,128]{1,0:T(8,128)S(1)}, f32[256,128]{1,0:T(8,128)S(1)}, f32[128,12...) custom-call(s32[512]{0:T(512)} %rows_hbm.1, ...), custom_call_target="tpu_custom_call" | custom-call | tf_op jit(solution)/shard_map/pallas_call | solution.py:327
  11.4 1.8 %collective-permute-start = (f32[256,128]{1,0:T(8,128)S(1)}, f32[256,128]{1,0:T(8,128)S(1)}, u32[]{:S(2)}, u32[]{:S(2)}) collective-permute-start(f32[256,128]{1,0:T(8,128)S(1)} %get-tuple-element.44), channel_id=1, source_target_pairs={{0,1},{1,0},{2,3},{3,2},{4,5},{5,4},{6,7},{7,6},{8,9},{9,8},{10,11... | collective-permute-start | bytes 393224 | tf_op jit(solution)/shard_map/ppermute | solution.py:384
  13.3 2.8 %collective-permute-start.3 = (f32[96,128]{1,0:T(8,128)S(1)}, f32[96,128]{1,0:T(8,128)S(1)}, u32[]{:S(2)}, u32[]{:S(2)}) collective-permute-start(f32[96,128]{1,0:T(8,128)S(1)} %get-tuple-element.50.own), channel_id=1, source_target_pairs={{0,64},{32,96},{64,0},{96,32},{1,65},{33,97},{65,1},{97,33},{2,66}... | collective-permute-start | bytes 147464 | tf_op jit(solution)/shard_map/ppermute | solution.py:396
  16.1 0.3 collective-permute-start.2
  16.4 2.4 %collective-permute-start.1 = (f32[96,128]{1,0:T(8,128)S(1)}, f32[96,128]{1,0:T(8,128)S(1)}, u32[]{:S(2)}, u32[]{:S(2)}) collective-permute-start(f32[96,128]{1,0:T(8,128)S(1)} %get-tuple-element.50.own), channel_id=1, source_target_pairs={{0,96},{32,0},{64,32},{96,64},{1,97},{33,1},{65,33},{97,65},{2,98}... | collective-permute-start | bytes 147464 | tf_op jit(solution)/shard_map/ppermute | solution.py:396
  18.8 0.0 collective-permute-done.3.second
  18.8 1.5 %collective-permute-done.2.third = f32[96,128]{1,0:T(8,128)S(1)} collective-permute-done((f32[96,128]{1,0:T(8,128)S(1)}, f32[96,128]{1,0:T(8,128)S(1)}, u32[]{:S(2)}, u32[]{:S(2)}) %collective-permute-start.2) | collective-permute-done | bytes 49184 | tf_op jit(solution)/shard_map/ppermute | solution.py:396
  20.2 0.0 collective-permute-done.1.first
  20.2 0.0 collective-permute-done
  20.3 14.1 %all_to_all.40 = f32[16,16,128]{2,1,0:T(8,128)S(1)} all-to-all(f32[16,16,128]{2,1,0:T(8,128)S(1)} %bitcast.34), channel_id=1, replica_groups={{0,2,4,6,8,10,12,14,16,18,20,22,24,26,28,30},{1,3,5,7,9,11,13,15,17,19,..., dimensions={0} | all-to-all | bytes 262144 | tf_op jit(solution)/shard_map/all_to_all | solution.py:390
  34.4 0.0 copy-done
  34.4 5.4 %shard_map.121 = (f32[256,128]{1,0:T(8,128)S(1)}, f32[272,128]{1,0:T(8,128)S(1)}, f32[128,128]{1,0:T(8,128)S(1)}, f32[64,128]{1,0:T(8,128)S(1)}) custom-call(s32[512]{0:T(512)S(1)} %get-tuple-element.40.rows, bf16[128,128,512]{2,1,0:T(8,128)(2,1)S(1)} %get-tuple-element.41.turned, f32[16,128]{1,0:T(8,128)S(1)} %fusion.1.own_scale, ...), custom_call_target="tpu_custom_call" | custom-call | flops 7000000000 | bytes 1048576 | tf_op jit(solution)/shard_map/pallas_call | solution.py:369
  39.7 3.0 %collective-permute-start.4 = (f32[272,128]{1,0:T(8,128)S(1)}, f32[272,128]{1,0:T(8,128)S(1)}, u32[]{:S(2)}, u32[]{:S(2)}) collective-permute-start(f32[272,128]{1,0:T(8,128)S(1)} %get-tuple-element.54), channel_id=1, source_target_pairs={{0,1},{1,0},{2,3},{3,2},{4,5},{5,4},{6,7},{7,6},{8,9},{9,8},{10,11... | collective-permute-start | bytes 417800 | tf_op jit(solution)/shard_map/ppermute | solution.py:384
  42.8 1.0 collective-permute-done.4
  43.9 12.3 %all_to_all.41 = f32[16,3,16,128]{3,2,1,0:T(8,128)S(1)} all-to-all(f32[16,3,16,128]{3,2,1,0:T(8,128)S(1)} %pad_maximum_fusion), channel_id=1, replica_groups={{0,2,4,6,8,10,12,14,16,18,20,22,24,26,28,30},{1,3,5,7,9,11,13,15,17,19,..., dimensions={0} | all-to-all | bytes 786432 | tf_op jit(solution)/shard_map/all_to_all | solution.py:390
  56.2 5.4 %shard_map.122 = (f32[128,128]{1,0:T(8,128)S(1)}, f32[72,128]{1,0:T(8,128)S(1)}, f32[16,128]{1,0:T(8,128)S(1)}) custom-call(s32[512]{0:T(512)S(1)} %get-tuple-element.40.rows, bf16[128,128,512]{2,1,0:T(8,128)(2,1)S(1)} %get-tuple-element.41.turned, f32[768,128]{1,0:T(8,128)S(1)} %bitcast.25, f32[16,128]{1,0:T(8,128)S(1)} %fusion.1.own_scale, ...), custom_call_target="tpu_custom_call" | custom-call | flops 7000000000 | bytes 1048576 | tf_op jit(solution)/shard_map/pallas_call | solution.py:369
  61.6 8.9 %all_to_all.42 = f32[4,72,128]{2,1,0:T(8,128)S(1)} all-to-all(f32[4,72,128]{2,1,0:T(8,128)S(1)} %broadcast_in_dim.5), channel_id=1, replica_groups=mesh['scen'=4,'arc'=32] {'scen'}, dimensions={0} | all-to-all | bytes 294912 | tf_op jit(solution)/shard_map/all_to_all | solution.py:402
  70.5 0.1 shard_map.123
  70.6 12.8 %all_to_all.43 = f32[32,1,128]{2,1,0:T(1,128)S(1)} all-to-all(f32[32,1,128]{2,1,0:T(1,128)S(1)} %bitcast.32), channel_id=1, replica_groups=mesh['scen'=4,'arc'=32] {'arc'}, dimensions={0} | all-to-all | bytes 32768 | tf_op jit(solution)/shard_map/all_to_all | solution.py:451
  83.4 4.0 %shard_map.124 = (f32[512,128]{1,0:T(8,128)S(1)}, f32[512,128]{1,0:T(8,128)S(1)}, f32[4,4096]{1,0:T(4,128)}, f32[8,128]{1,0:T(8,128)S(1)}) custom-call(s32[512]{0:T(512)S(1)} %get-tuple-element.40.rows, bf16[128,128,512]{2,1,0:T(8,128)(2,1)S(1)} %get-tuple-element.41.turned, f32[1,128]{1,0:T(1,128)S(1)} %broadcast_in_dim.4.step_size, ...), custom_call_target="tpu_custom_call" | custom-call | flops 7000000000 | bytes 1048576 | tf_op jit(solution)/shard_map/pallas_call | solution.py:369
  87.5 0.6 collective-permute-start.5
  88.1 1.2 %collective-permute-done.5 = f32[512,128]{1,0:T(8,128)S(1)} collective-permute-done((f32[512,128]{1,0:T(8,128)S(1)}, f32[512,128]{1,0:T(8,128)S(1)}, u32[]{:S(2)}, u32[]{:S(2)}) %collective-permute-start.5) | collective-permute-done | bytes 262176 | tf_op jit(solution)/shard_map/ppermute | solution.py:384
  89.3 10.9 %all_to_all.44 = f32[16,32,128]{2,1,0:T(8,128)S(1)} all-to-all(f32[16,32,128]{2,1,0:T(8,128)S(1)} %bitcast.33), channel_id=1, replica_groups={{0,2,4,6,8,10,12,14,16,18,20,22,24,26,28,30},{1,3,5,7,9,11,13,15,17,19,..., dimensions={0} | all-to-all | bytes 524288 | tf_op jit(solution)/shard_map/all_to_all | solution.py:390
  100.2 0.6 shard_map.125
  100.8 14.0 %all_to_all.45 = f32[128,1,128]{2,1,0:T(1,128)S(1)} all-to-all(f32[128,1,128]{2,1,0:T(1,128)S(1)} %bitcast.26), channel_id=1, replica_groups=mesh['scen'=4,'arc'=32] {'scen','arc'}, dimensions={0} | all-to-all | bytes 131072 | tf_op jit(solution)/shard_map/all_to_all | solution.py:464
  114.8 0.2 reduce_sum.9
  115.0 0.6 fusion.2
  (10 shorter events, 0.1 us)
Async XLA Ops:
  0.6 33.7 %copy-start = (s32[4096]{0:T(1024)S(1)}, s32[4096]{0:T(1024)}, u32[]{:S(2)}) copy-start(s32[4096]{0:T(1024)} %param.12) | copy-start | bytes 49156
  11.4 8.8 %collective-permute-start = (f32[256,128]{1,0:T(8,128)S(1)}, f32[256,128]{1,0:T(8,128)S(1)}, u32[]{:S(2)}, u32[]{:S(2)}) collective-permute-start(f32[256,128]{1,0:T(8,128)S(1)} %get-tuple-element.44), channel_id=1, source_target_pairs={{0,1},{1,0},{2,3},{3,2},{4,5},{5,4},{6,7},{7,6},{8,9},{9,8},{10,11... | collective-permute-start | bytes 393224 | tf_op jit(solution)/shard_map/ppermute | solution.py:384
  13.3 5.5 %collective-permute-start.3 = (f32[96,128]{1,0:T(8,128)S(1)}, f32[96,128]{1,0:T(8,128)S(1)}, u32[]{:S(2)}, u32[]{:S(2)}) collective-permute-start(f32[96,128]{1,0:T(8,128)S(1)} %get-tuple-element.50.own), channel_id=1, source_target_pairs={{0,64},{32,96},{64,0},{96,32},{1,65},{33,97},{65,1},{97,33},{2,66}... | collective-permute-start | bytes 147464 | tf_op jit(solution)/shard_map/ppermute | solution.py:396
  16.1 4.2 %collective-permute-start.2 = (f32[96,128]{1,0:T(8,128)S(1)}, f32[96,128]{1,0:T(8,128)S(1)}, u32[]{:S(2)}, u32[]{:S(2)}) collective-permute-start(f32[96,128]{1,0:T(8,128)S(1)} %get-tuple-element.50.own), channel_id=1, source_target_pairs={{0,32},{32,64},{64,96},{96,0},{1,33},{33,65},{65,97},{97,1},{2,34}... | collective-permute-start | bytes 147464 | tf_op jit(solution)/shard_map/ppermute | solution.py:396
  16.4 3.8 %collective-permute-start.1 = (f32[96,128]{1,0:T(8,128)S(1)}, f32[96,128]{1,0:T(8,128)S(1)}, u32[]{:S(2)}, u32[]{:S(2)}) collective-permute-start(f32[96,128]{1,0:T(8,128)S(1)} %get-tuple-element.50.own), channel_id=1, source_target_pairs={{0,96},{32,0},{64,32},{96,64},{1,97},{33,1},{65,33},{97,65},{2,98}... | collective-permute-start | bytes 147464 | tf_op jit(solution)/shard_map/ppermute | solution.py:396
  39.7 4.0 %collective-permute-start.4 = (f32[272,128]{1,0:T(8,128)S(1)}, f32[272,128]{1,0:T(8,128)S(1)}, u32[]{:S(2)}, u32[]{:S(2)}) collective-permute-start(f32[272,128]{1,0:T(8,128)S(1)} %get-tuple-element.54), channel_id=1, source_target_pairs={{0,1},{1,0},{2,3},{3,2},{4,5},{5,4},{6,7},{7,6},{8,9},{9,8},{10,11... | collective-permute-start | bytes 417800 | tf_op jit(solution)/shard_map/ppermute | solution.py:384
  87.5 1.8 %collective-permute-start.5 = (f32[512,128]{1,0:T(8,128)S(1)}, f32[512,128]{1,0:T(8,128)S(1)}, u32[]{:S(2)}, u32[]{:S(2)}) collective-permute-start(f32[512,128]{1,0:T(8,128)S(1)} %get-tuple-element.69), channel_id=1, source_target_pairs={{0,1},{1,0},{2,3},{3,2},{4,5},{5,4},{6,7},{7,6},{8,9},{9,8},{10,11... | collective-permute-start | bytes 786440 | tf_op jit(solution)/shard_map/ppermute | solution.py:384
